TPU v7x, 128 devices: a whole 4x4x4 slice. The times are simulated.
128 devices in a mesh: gx: 4 (over z), gy: 8 (over y, core), gz: 4 (over x).
Axes of the slice: x: 4, y: 4, z: 4, core: 2. Of those that a mesh axis runs over, the one named last changes fastest.
Arguments:
- density: float32 [256, 2048, 1024], P('gz', 'gy', 'gx'), may hold values from 0 to 1
- depth_rank: int32 [4], replicated, may hold values from 0 to 15, as said below
- knots: int32 [8], replicated, may hold values from 0 to 255, as said below
- tf_color: float32 [3, 8], replicated, may hold values from 0.1 to 1
- tf_sigma: float32 [8], replicated, may hold values from 0.25 to 6
Outputs:
- image: float32 [8, 2048, 1024], P(None, ('gy', 'gz'), 'gx')
Inputs may be any that keep to these rules, and one draw needn't show every extreme that they name: `depth_rank`: strictly increasing or strictly decreasing along the slabs, the ends being 0 and 15. `knots`: strictly increasing, the first 0 and the last 255.
All inputs are finite; a program needn't handle non-finite values.
Results may differ from a plain program's by a relative error of at most 0.0003.
Values sent between devices are 32-bit elements; how exact they have to be, the bound alone decides.
No kernel may reach another device: no remote copies, remote signals or barrier semaphores. Data moves between devices by JAX's collectives and lax.ppermute only.
A program may use at most 128 MiB of HBM per device.

v0:
```python
import jax
import jax.numpy as jnp
from jax import lax
from jax.sharding import PartitionSpec as P

BINS = 256


def padded_2(array, sides, width):
    for axis, dim in sides:
        peers, length = (lax.axis_size(axis), array.shape[dim])
        up = [(i, (i + 1) % peers) for i in range(peers - 1)]
        down = [(j, i) for i, j in up]
        last = lax.slice_in_dim(array, length - width, length, axis=dim)
        leading = lax.slice_in_dim(array, 0, width, axis=dim)
        before = lax.ppermute(last, axis, up)
        after = lax.ppermute(leading, axis, down)
        array = jnp.concatenate([before, array, after], axis=dim)
    return array


def from_partner(array, axis, distance):
    return lax.ppermute(array, axis, [(i, i ^ 1 << distance) for i in range(lax.axis_size(axis))])


def transfer(position, knots, tf_color, tf_sigma):
    knot_pos = knots.astype(jnp.float32)
    earlier = jnp.concatenate([knot_pos[:1] - 1.0, knot_pos[:-1]])
    later = jnp.concatenate([knot_pos[1:], knot_pos[-1:] + 1.0])
    sigma = jnp.zeros_like(position)
    red = jnp.zeros_like(position)
    green = jnp.zeros_like(position)
    blue = jnp.zeros_like(position)
    for index in range(knots.shape[0]):
        rising = jnp.clip(
            (position - earlier[index]) / (knot_pos[index] - earlier[index]), 0.0, 1.0
        )
        falling = jnp.clip((later[index] - position) / (later[index] - knot_pos[index]), 0.0, 1.0)
        hat_value = jnp.minimum(rising, falling)
        sigma = sigma + hat_value * tf_sigma[index]
        red = red + hat_value * tf_color[0, index]
        green = green + hat_value * tf_color[1, index]
        blue = blue + hat_value * tf_color[2, index]
    return (sigma, red, green, blue)


def samples(slab, knots, tf_color, tf_sigma, inv_depth):
    center = slab[1:-1, 1:-1, 1:-1]
    grad_x = slab[1:-1, 1:-1, 2:] - slab[1:-1, 1:-1, :-2]
    grad_y = slab[1:-1, 2:, 1:-1] - slab[1:-1, :-2, 1:-1]
    grad_z = slab[2:, 1:-1, 1:-1] - slab[:-2, 1:-1, 1:-1]
    length = jnp.sqrt(grad_x * grad_x + grad_y * grad_y + grad_z * grad_z)
    factor = 1.0 / jnp.maximum(length, 0.5)
    normal_x = grad_x * factor
    normal_y = grad_y * factor
    normal_z = grad_z * factor
    shade = 0.3 + 0.7 * jnp.abs(0.48 * normal_x + 0.6 * normal_y + 0.64 * normal_z)
    sigma, red, green, blue = transfer(center * (BINS - 1.0), knots, tf_color, tf_sigma)
    tau = sigma * inv_depth
    return (tau, (red * shade, green * shade, blue * shade, normal_x, normal_y, normal_z))


def over(front, back):
    return front + (1.0 - front[3:4]) * back


def body(density, depth_rank, knots, tf_color, tf_sigma):
    depth_local, rows_local, cols_local = density.shape
    groups = lax.axis_size("gz")
    myself = lax.axis_index("gz")
    inv_depth = 1.0 / (depth_local * groups)
    forward = depth_rank[0] < depth_rank[depth_rank.shape[0] - 1]
    padded = padded_2(density, (("gx", 2), ("gy", 1), ("gz", 0)), 1)
    block = 16
    count = depth_local // block
    zero_index = jnp.zeros((), jnp.int32)

    def march(step, carry):
        picture, optical = carry
        which = jnp.where(forward, step, count - 1 - step).astype(jnp.int32)
        slab = lax.dynamic_slice(
            padded,
            (which * block, zero_index, zero_index),
            (block + 2, rows_local + 2, cols_local + 2),
        )
        tau, feats = samples(slab, knots, tf_color, tf_sigma, inv_depth)
        running = jnp.cumsum(tau, axis=0)
        whole = running[-1]
        before = jnp.where(forward, running - tau, whole - running)
        weight = jnp.exp(-(optical + before)) * (1.0 - jnp.exp(-tau))
        offset = (myself * depth_local + which * block).astype(jnp.float32)
        zpos = (offset + jnp.arange(block, dtype=jnp.float32) + 0.5) * inv_depth
        depth = jnp.where(forward, zpos, 1.0 - zpos)[:, None, None]
        layers = jnp.stack(
            [
                jnp.sum(weight * feats[0], axis=0),
                jnp.sum(weight * feats[1], axis=0),
                jnp.sum(weight * feats[2], axis=0),
                jnp.sum(weight, axis=0),
                jnp.sum(weight * depth, axis=0),
                jnp.sum(weight * feats[3], axis=0),
                jnp.sum(weight * feats[4], axis=0),
                jnp.sum(weight * feats[5], axis=0),
            ]
        )
        return (picture + layers, optical + whole)

    start = (
        jnp.zeros((8, rows_local, cols_local), jnp.float32),
        jnp.zeros((rows_local, cols_local), jnp.float32),
    )
    partial_image, _ = lax.fori_loop(0, count, march, start)
    piece_rows = rows_local // groups
    current = partial_image.reshape(8, groups, piece_rows, cols_local)
    for level in range(groups.bit_length() - 1):
        remaining = current.shape[1]
        paired = current.reshape(8, remaining // 2, 2, piece_rows, cols_local)
        mybit = myself >> level & 1
        keep = jnp.where(mybit == 1, paired[:, :, 1], paired[:, :, 0])
        outgoing = jnp.where(mybit == 1, paired[:, :, 0], paired[:, :, 1])
        incoming = from_partner(outgoing, "gz", level)
        partner = jnp.bitwise_xor(myself, 1 << level)
        mine_first = depth_rank[myself] < depth_rank[partner]
        front = jnp.where(mine_first, keep, incoming)
        back = jnp.where(mine_first, incoming, keep)
        current = over(front, back)
    return current.reshape(8, piece_rows, cols_local)


def solution(mesh):
    in_specs = (P("gz", "gy", "gx"), P(), P(), P(), P())
    out_specs = P(None, ("gy", "gz"), "gx")
    return jax.shard_map(body, mesh=mesh, in_specs=in_specs, out_specs=out_specs, check_vma=False)
```

profile of v0, /device:TPU:40, one launch (start us, length us, event | category | flops | bytes accessed | tf_op | source)
XLA Modules:
  0.0 739.9 jit_solution(572242734811889024)
XLA Ops:
  67.5 26.9 %pad_maximum_fusion = f32[66,258,258]{2,1,0:T(8,128)} fusion(f32[1,258,258]{2,1,0:T(8,128)S(1)} %collective-permute-done.5, f32[64,1,258]{2,1,0:T(1,128)S(1)} %collective-permute-done.3, f32[64,256,1]{2,1,0:T(8,128)} %copy.17, f32[64,256,256]{2,1,0:T(8,128)} %param.7, f32[64,256,1]{2,1,0:T(8,128)} %copy.16, f32[64,1,258]{2,1,0:T(1,128)S(1)} %collective-permute-done.2, ...), kind=kLoop, calls=%fused_computation.36 | loop fusion | flops 26359344 | bytes 35145792 | tf_op jit(solution)/shard_map/concatenate | solution.py:18
  94.4 600.3 %while.19 = (s32[]{:T(128)}, f32[8,256,256]{2,1,0:T(8,128)S(1)}, f32[256,256]{1,0:T(8,128)S(1)}, pred[]{:T(512)}, f32[66,258,258]{2,1,0:T(8,128)}, /*index=5*/f3...) while((s32[]{:T(128)}, f32[8,256,256]{2,1,0:T(8,128)S(1)}, ...), condition=%wide.region_10.11_spmd.clone, body=%wide.region_0.10_spmd.clone.sunk | while | flops 455737440 | bytes 123747120 | solution.py:112
  95.3 27.7 %fusion.22 = f32[16,256,256]{2,1,0:T(8,128)} fusion(f32[]{:T(128)} %bitcast.200, f32[]{:T(128)} %bitcast.201, f32[]{:T(128)} %bitcast.202, f32[]{:T(128)} %bitcast.203, f32[]{:T(128)} %bitcast.204, f32[]{:T(128)} %bitcast.205, f32[]{:T(128)} %bitcast.206, f32[]{:T(128)} %bitcast.207, f32[]{:T(128)} %get-tuple-element.816, f32[]{:T(128)} %bitcast.208, ...), kind=kOutput, calls=%fused_computation.66.clone.1 | output fusion | flops 92274688 | bytes 8402440 | tf_op jit(solution)/shard_map/while/body/eval_jaxpr/jit(cumsum)/reduce_window_sum | solution.py:87
  125.0 38.8 %multiply_reduce_fusion.11 = (f32[256,256]{1,0:T(8,128)S(1)}, f32[256,256]{1,0:T(8,128)S(1)}, f32[256,256]{1,0:T(8,128)S(1)}, f32[256,256]{1,0:T(8,128)S(1)}, f3...) fusion(f32[16]{0:T(128)S(1)} %broadcast_select_fusion.6, ...), kind=kLoop, calls=%fused_computation.4.clone.1 | loop fusion | flops 107675648 | bytes 52166848 | tf_op jit(solution)/shard_map/while/body/eval_jaxpr/reduce_sum | solution.py:103
  164.5 27.4 %multiply_reduce_fusion.12 = (f32[256,256]{1,0:T(8,128)S(1)}, f32[16,256,256]{2,1,0:T(8,128)S(1)}) fusion(f32[16,256,256]{2,1,0:T(8,128)S(1)} %get-tuple-element.718, f32[]{:T(128)} %bitcast.218, f32[]{:T(128)} %bitcast.219, f32[]{:T(128)} %bitcast.220, f32[]{:T(128)} %bitcast.221, f32[]{:T(128)} %bitcast.222, f32[]{:T(128)} %bitcast.223, ...), kind=kLoop, calls=%fused_computation.8.clone.1 | loop fusion | flops 97452032 | bytes 25428084 | tf_op jit(solution)/shard_map/while/body/eval_jaxpr/reduce_sum | solution.py:98
  191.9 25.9 %multiply_reduce_fusion.14 = f32[256,256]{1,0:T(8,128)S(1)} fusion(f32[16,256,256]{2,1,0:T(8,128)S(1)} %get-tuple-element.718, f32[16,256,256]{2,1,0:T(8,128)S(1)} %get-tuple-element.730, f32[]{:T(128)} %bitcast.234, f32[]{:T(128)} %bitcast.235, f32[]{:T(128)} %bitcast.236, f32[]{:T(128)} %bitcast.237, f32[]{:T(128)} %bitcast.238, f32[]{:T(128)} %bitcast.239, ...), kind=kLoop, calls=%fused_computation.9.clone.1 | loop fusion | flops 78577664 | bytes 12845172 | tf_op jit(solution)/shard_map/while/body/eval_jaxpr/reduce_sum | solution.py:97
  218.5 25.8 %multiply_reduce_fusion.13 = f32[256,256]{1,0:T(8,128)S(1)} fusion(f32[16,256,256]{2,1,0:T(8,128)S(1)} %get-tuple-element.718, f32[16,256,256]{2,1,0:T(8,128)S(1)} %get-tuple-element.730, f32[]{:T(128)} %bitcast.226, f32[]{:T(128)} %bitcast.227, f32[]{:T(128)} %bitcast.228, f32[]{:T(128)} %bitcast.229, f32[]{:T(128)} %bitcast.230, f32[]{:T(128)} %bitcast.231, ...), kind=kLoop, calls=%fused_computation.10.clone.1 | loop fusion | flops 78577664 | bytes 12845172 | tf_op jit(solution)/shard_map/while/body/eval_jaxpr/reduce_sum | solution.py:96
  245.9 27.6 %fusion.22 = f32[16,256,256]{2,1,0:T(8,128)} fusion(f32[]{:T(128)} %bitcast.200, f32[]{:T(128)} %bitcast.201, f32[]{:T(128)} %bitcast.202, f32[]{:T(128)} %bitcast.203, f32[]{:T(128)} %bitcast.204, f32[]{:T(128)} %bitcast.205, f32[]{:T(128)} %bitcast.206, f32[]{:T(128)} %bitcast.207, f32[]{:T(128)} %get-tuple-element.816, f32[]{:T(128)} %bitcast.208, ...), kind=kOutput, calls=%fused_computation.66.clone.1 | output fusion | flops 92274688 | bytes 8402440 | tf_op jit(solution)/shard_map/while/body/eval_jaxpr/jit(cumsum)/reduce_window_sum | solution.py:87
  275.6 38.3 %multiply_reduce_fusion.11 = (f32[256,256]{1,0:T(8,128)S(1)}, f32[256,256]{1,0:T(8,128)S(1)}, f32[256,256]{1,0:T(8,128)S(1)}, f32[256,256]{1,0:T(8,128)S(1)}, f3...) fusion(f32[16]{0:T(128)S(1)} %broadcast_select_fusion.6, ...), kind=kLoop, calls=%fused_computation.4.clone.1 | loop fusion | flops 107675648 | bytes 52166848 | tf_op jit(solution)/shard_map/while/body/eval_jaxpr/reduce_sum | solution.py:103
  314.6 27.4 %multiply_reduce_fusion.12 = (f32[256,256]{1,0:T(8,128)S(1)}, f32[16,256,256]{2,1,0:T(8,128)S(1)}) fusion(f32[16,256,256]{2,1,0:T(8,128)S(1)} %get-tuple-element.718, f32[]{:T(128)} %bitcast.218, f32[]{:T(128)} %bitcast.219, f32[]{:T(128)} %bitcast.220, f32[]{:T(128)} %bitcast.221, f32[]{:T(128)} %bitcast.222, f32[]{:T(128)} %bitcast.223, ...), kind=kLoop, calls=%fused_computation.8.clone.1 | loop fusion | flops 97452032 | bytes 25428084 | tf_op jit(solution)/shard_map/while/body/eval_jaxpr/reduce_sum | solution.py:98
  342.0 25.9 %multiply_reduce_fusion.14 = f32[256,256]{1,0:T(8,128)S(1)} fusion(f32[16,256,256]{2,1,0:T(8,128)S(1)} %get-tuple-element.718, f32[16,256,256]{2,1,0:T(8,128)S(1)} %get-tuple-element.730, f32[]{:T(128)} %bitcast.234, f32[]{:T(128)} %bitcast.235, f32[]{:T(128)} %bitcast.236, f32[]{:T(128)} %bitcast.237, f32[]{:T(128)} %bitcast.238, f32[]{:T(128)} %bitcast.239, ...), kind=kLoop, calls=%fused_computation.9.clone.1 | loop fusion | flops 78577664 | bytes 12845172 | tf_op jit(solution)/shard_map/while/body/eval_jaxpr/reduce_sum | solution.py:97
  368.5 25.8 %multiply_reduce_fusion.13 = f32[256,256]{1,0:T(8,128)S(1)} fusion(f32[16,256,256]{2,1,0:T(8,128)S(1)} %get-tuple-element.718, f32[16,256,256]{2,1,0:T(8,128)S(1)} %get-tuple-element.730, f32[]{:T(128)} %bitcast.226, f32[]{:T(128)} %bitcast.227, f32[]{:T(128)} %bitcast.228, f32[]{:T(128)} %bitcast.229, f32[]{:T(128)} %bitcast.230, f32[]{:T(128)} %bitcast.231, ...), kind=kLoop, calls=%fused_computation.10.clone.1 | loop fusion | flops 78577664 | bytes 12845172 | tf_op jit(solution)/shard_map/while/body/eval_jaxpr/reduce_sum | solution.py:96
  396.0 27.6 %fusion.22 = f32[16,256,256]{2,1,0:T(8,128)} fusion(f32[]{:T(128)} %bitcast.200, f32[]{:T(128)} %bitcast.201, f32[]{:T(128)} %bitcast.202, f32[]{:T(128)} %bitcast.203, f32[]{:T(128)} %bitcast.204, f32[]{:T(128)} %bitcast.205, f32[]{:T(128)} %bitcast.206, f32[]{:T(128)} %bitcast.207, f32[]{:T(128)} %get-tuple-element.816, f32[]{:T(128)} %bitcast.208, ...), kind=kOutput, calls=%fused_computation.66.clone.1 | output fusion | flops 92274688 | bytes 8402440 | tf_op jit(solution)/shard_map/while/body/eval_jaxpr/jit(cumsum)/reduce_window_sum | solution.py:87
  425.6 39.2 %multiply_reduce_fusion.11 = (f32[256,256]{1,0:T(8,128)S(1)}, f32[256,256]{1,0:T(8,128)S(1)}, f32[256,256]{1,0:T(8,128)S(1)}, f32[256,256]{1,0:T(8,128)S(1)}, f3...) fusion(f32[16]{0:T(128)S(1)} %broadcast_select_fusion.6, ...), kind=kLoop, calls=%fused_computation.4.clone.1 | loop fusion | flops 107675648 | bytes 52166848 | tf_op jit(solution)/shard_map/while/body/eval_jaxpr/reduce_sum | solution.py:103
  465.5 27.4 %multiply_reduce_fusion.12 = (f32[256,256]{1,0:T(8,128)S(1)}, f32[16,256,256]{2,1,0:T(8,128)S(1)}) fusion(f32[16,256,256]{2,1,0:T(8,128)S(1)} %get-tuple-element.718, f32[]{:T(128)} %bitcast.218, f32[]{:T(128)} %bitcast.219, f32[]{:T(128)} %bitcast.220, f32[]{:T(128)} %bitcast.221, f32[]{:T(128)} %bitcast.222, f32[]{:T(128)} %bitcast.223, ...), kind=kLoop, calls=%fused_computation.8.clone.1 | loop fusion | flops 97452032 | bytes 25428084 | tf_op jit(solution)/shard_map/while/body/eval_jaxpr/reduce_sum | solution.py:98
  492.9 25.9 %multiply_reduce_fusion.14 = f32[256,256]{1,0:T(8,128)S(1)} fusion(f32[16,256,256]{2,1,0:T(8,128)S(1)} %get-tuple-element.718, f32[16,256,256]{2,1,0:T(8,128)S(1)} %get-tuple-element.730, f32[]{:T(128)} %bitcast.234, f32[]{:T(128)} %bitcast.235, f32[]{:T(128)} %bitcast.236, f32[]{:T(128)} %bitcast.237, f32[]{:T(128)} %bitcast.238, f32[]{:T(128)} %bitcast.239, ...), kind=kLoop, calls=%fused_computation.9.clone.1 | loop fusion | flops 78577664 | bytes 12845172 | tf_op jit(solution)/shard_map/while/body/eval_jaxpr/reduce_sum | solution.py:97
  519.4 25.8 %multiply_reduce_fusion.13 = f32[256,256]{1,0:T(8,128)S(1)} fusion(f32[16,256,256]{2,1,0:T(8,128)S(1)} %get-tuple-element.718, f32[16,256,256]{2,1,0:T(8,128)S(1)} %get-tuple-element.730, f32[]{:T(128)} %bitcast.226, f32[]{:T(128)} %bitcast.227, f32[]{:T(128)} %bitcast.228, f32[]{:T(128)} %bitcast.229, f32[]{:T(128)} %bitcast.230, f32[]{:T(128)} %bitcast.231, ...), kind=kLoop, calls=%fused_computation.10.clone.1 | loop fusion | flops 78577664 | bytes 12845172 | tf_op jit(solution)/shard_map/while/body/eval_jaxpr/reduce_sum | solution.py:96
  546.9 27.1 %fusion.22 = f32[16,256,256]{2,1,0:T(8,128)} fusion(f32[]{:T(128)} %bitcast.200, f32[]{:T(128)} %bitcast.201, f32[]{:T(128)} %bitcast.202, f32[]{:T(128)} %bitcast.203, f32[]{:T(128)} %bitcast.204, f32[]{:T(128)} %bitcast.205, f32[]{:T(128)} %bitcast.206, f32[]{:T(128)} %bitcast.207, f32[]{:T(128)} %get-tuple-element.816, f32[]{:T(128)} %bitcast.208, ...), kind=kOutput, calls=%fused_computation.66.clone.1 | output fusion | flops 92274688 | bytes 8402440 | tf_op jit(solution)/shard_map/while/body/eval_jaxpr/jit(cumsum)/reduce_window_sum | solution.py:87
  576.0 37.4 %multiply_reduce_fusion.11 = (f32[256,256]{1,0:T(8,128)S(1)}, f32[256,256]{1,0:T(8,128)S(1)}, f32[256,256]{1,0:T(8,128)S(1)}, f32[256,256]{1,0:T(8,128)S(1)}, f3...) fusion(f32[16]{0:T(128)S(1)} %broadcast_select_fusion.6, ...), kind=kLoop, calls=%fused_computation.4.clone.1 | loop fusion | flops 107675648 | bytes 52166848 | tf_op jit(solution)/shard_map/while/body/eval_jaxpr/reduce_sum | solution.py:103
  614.1 27.4 %multiply_reduce_fusion.12 = (f32[256,256]{1,0:T(8,128)S(1)}, f32[16,256,256]{2,1,0:T(8,128)S(1)}) fusion(f32[16,256,256]{2,1,0:T(8,128)S(1)} %get-tuple-element.718, f32[]{:T(128)} %bitcast.218, f32[]{:T(128)} %bitcast.219, f32[]{:T(128)} %bitcast.220, f32[]{:T(128)} %bitcast.221, f32[]{:T(128)} %bitcast.222, f32[]{:T(128)} %bitcast.223, ...), kind=kLoop, calls=%fused_computation.8.clone.1 | loop fusion | flops 97452032 | bytes 25428084 | tf_op jit(solution)/shard_map/while/body/eval_jaxpr/reduce_sum | solution.py:98
  641.5 25.9 %multiply_reduce_fusion.14 = f32[256,256]{1,0:T(8,128)S(1)} fusion(f32[16,256,256]{2,1,0:T(8,128)S(1)} %get-tuple-element.718, f32[16,256,256]{2,1,0:T(8,128)S(1)} %get-tuple-element.730, f32[]{:T(128)} %bitcast.234, f32[]{:T(128)} %bitcast.235, f32[]{:T(128)} %bitcast.236, f32[]{:T(128)} %bitcast.237, f32[]{:T(128)} %bitcast.238, f32[]{:T(128)} %bitcast.239, ...), kind=kLoop, calls=%fused_computation.9.clone.1 | loop fusion | flops 78577664 | bytes 12845172 | tf_op jit(solution)/shard_map/while/body/eval_jaxpr/reduce_sum | solution.py:97
  668.0 25.8 %multiply_reduce_fusion.13 = f32[256,256]{1,0:T(8,128)S(1)} fusion(f32[16,256,256]{2,1,0:T(8,128)S(1)} %get-tuple-element.718, f32[16,256,256]{2,1,0:T(8,128)S(1)} %get-tuple-element.730, f32[]{:T(128)} %bitcast.226, f32[]{:T(128)} %bitcast.227, f32[]{:T(128)} %bitcast.228, f32[]{:T(128)} %bitcast.229, f32[]{:T(128)} %bitcast.230, f32[]{:T(128)} %bitcast.231, ...), kind=kLoop, calls=%fused_computation.10.clone.1 | loop fusion | flops 78577664 | bytes 12845172 | tf_op jit(solution)/shard_map/while/body/eval_jaxpr/reduce_sum | solution.py:96
  699.9 22.4 %collective-permute-done.6 = f32[8,2,64,256]{3,2,1,0:T(8,128)S(1)} collective-permute-done((f32[8,2,64,256]{3,2,1,0:T(8,128)}, f32[8,2,64,256]{3,2,1,0:T(8,128)S(1)}, u32[]{:S(2)}, u32[]{:S(2)}) %collective-permute-start.6) | collective-permute-done | bytes 1048608 | tf_op jit(solution)/shard_map/ppermute | solution.py:23
  727.9 10.9 %collective-permute-done.7 = f32[8,1,64,256]{3,2,0,1:T(8,128)S(1)} collective-permute-done((f32[8,1,64,256]{3,2,0,1:T(8,128)S(1)}, f32[8,1,64,256]{3,2,0,1:T(8,128)S(1)}, u32[]{:S(2)}, u32[]{:S(2)}) %collective-permute-start.7) | collective-permute-done | bytes 524320 | tf_op jit(solution)/shard_map/ppermute | solution.py:23
  (104 shorter events, 83.8 us)
Async XLA Ops:
  15.9 11.1 %collective-permute-start = (f32[64,256,1]{1,0,2:T(8,128)S(1)}, f32[64,256,1]{1,0,2:T(8,128)S(1)}, u32[]{:S(2)}, u32[]{:S(2)}) collective-permute-start(f32[64,256,1]{1,0,2:T(8,128)S(1)} %copy.26), channel_id=1, source_target_pairs={{0,32},{32,64},{64,96},{1,33},{33,65},{65,97},{2,34},{34,66},{66,9... | collective-permute-start | bytes 196616 | tf_op jit(solution)/shard_map/ppermute | solution.py:16
  25.0 6.7 collective-permute-start.1
  36.3 10.2 %copy-start = (f32[64,256,1]{2,1,0:T(8,128)S(1)}, f32[64,256,1]{2,1,0:T(8,128)}, u32[]{:S(2)}) copy-start(f32[64,256,1]{2,1,0:T(8,128)} %copy.17) | copy-start | bytes 196612
  38.6 6.1 collective-permute-start.2
  40.7 13.0 %copy-start.4 = (s32[8]{0:T(128)S(1)}, s32[8]{0:T(128)}, u32[]{:S(2)}) copy-start(s32[8]{0:T(128)} %param.9) | copy-start | bytes 100
  40.7 24.7 %copy-start.3 = (s32[4]{0:T(128)S(1)}, s32[4]{0:T(128)}, u32[]{:S(2)}) copy-start(s32[4]{0:T(128)} %param.8) | copy-start | bytes 52
  40.7 5.8 collective-permute-start.3
  48.9 18.6 %collective-permute-start.4 = (f32[1,258,258]{2,1,0:T(8,128)}, f32[1,258,258]{2,1,0:T(8,128)S(1)}, u32[]{:S(2)}, u32[]{:S(2)}) collective-permute-start(f32[1,258,258]{2,1,0:T(8,128)} %get-tuple-element.508), channel_id=1, source_target_pairs={{0,1},{1,2},{2,3},{4,5},{5,6},{6,7},{8,9},{9,10},{10,11},{12,13},{... | collective-permute-start | bytes 798776 | tf_op jit(solution)/shard_map/ppermute | solution.py:16
  52.3 15.2 %collective-permute-start.5 = (f32[1,258,258]{2,1,0:T(8,128)}, f32[1,258,258]{2,1,0:T(8,128)S(1)}, u32[]{:S(2)}, u32[]{:S(2)}) collective-permute-start(f32[1,258,258]{2,1,0:T(8,128)} %get-tuple-element.509), channel_id=1, source_target_pairs={{1,0},{2,1},{3,2},{5,4},{6,5},{7,6},{9,8},{10,9},{11,10},{13,12},{... | collective-permute-start | bytes 798776 | tf_op jit(solution)/shard_map/ppermute | solution.py:17
  67.4 26.9 %copy-start.1 = (f32[3,8]{1,0:T(4,128)S(1)}, f32[3,8]{1,0:T(4,128)}, u32[]{:S(2)}) copy-start(f32[3,8]{1,0:T(4,128)} %param.10) | copy-start | bytes 292
  67.4 26.9 %copy-start.2 = (f32[8]{0:T(128)S(1)}, f32[8]{0:T(128)}, u32[]{:S(2)}) copy-start(f32[8]{0:T(128)} %param.11) | copy-start | bytes 100
  695.9 26.4 %collective-permute-start.6 = (f32[8,2,64,256]{3,2,1,0:T(8,128)}, f32[8,2,64,256]{3,2,1,0:T(8,128)S(1)}, u32[]{:S(2)}, u32[]{:S(2)}) collective-permute-start(f32[8,2,64,256]{3,2,1,0:T(8,128)} %select_bitcast_fusion), channel_id=1, source_target_pairs={{0,1},{1,0},{2,3},{3,2},{4,5},{5,4},{6,7},{7,6},{8,9},{9,8},{10,11... | collective-permute-start | bytes 3145736 | tf_op jit(solution)/shard_map/ppermute | solution.py:23
  722.8 16.0 %collective-permute-start.7 = (f32[8,1,64,256]{3,2,0,1:T(8,128)S(1)}, f32[8,1,64,256]{3,2,0,1:T(8,128)S(1)}, u32[]{:S(2)}, u32[]{:S(2)}) collective-permute-start(f32[8,1,64,256]{3,2,0,1:T(8,128)S(1)} %select_bitcast_fusion.1), channel_id=1, source_target_pairs={{0,2},{1,3},{2,0},{3,1},{4,6},{5,7},{6,4},{7,5},{8,10},{9,11},{10,... | collective-permute-start | bytes 1572872 | tf_op jit(solution)/shard_map/ppermute | solution.py:23
where the time goes:
time: 744 us; the launch traced here: 740 us
  other arithmetic  621 us (83%)
  local copies, waits for them, and re-layouts  44.8 us (6%)
  waiting for transfers between devices  35.6 us (5%)
  starting transfers between devices  22.7 us (3%)
  between operations  15.2 us (2%)
    reduce_sum x4, other arithmetic, march(): jnp.sum(weight * feats[5], axis=0)  154 us
    another operation x4, other arithmetic, march(): running = jnp.cumsum(tau, axis=0)  110 us
    reduce_sum x4, other arithmetic, march(): jnp.sum(weight * feats[2], axis=0)  110 us
    reduce_sum x4, other arithmetic, march(): jnp.sum(weight * feats[1], axis=0)  103 us
    reduce_sum x4, other arithmetic, march(): jnp.sum(weight * feats[0], axis=0)  103 us
    ppermute x2, waiting for transfers between devices, from_partner(): lax.ppermute(array, axis, [(i, i ^ 1 << distance) for i in range(lax.axis...  33.4 us
    concatenate x1, other arithmetic, padded_2(): array = jnp.concatenate([before, array, after], axis=dim)  26.9 us
  transfers between devices with their start and end apart: 8, of which 4 were waited for; matrix products, arithmetic and copies ran while one was open for 2% of the time, Pallas kernels for 0%

commit v1 on v0

v1 whole, which is shorter than its diff:
```python
import jax
import jax.numpy as jnp
from jax import lax
from jax.experimental import pallas as pl
from jax.experimental.pallas import tpu as pltpu
from jax.sharding import PartitionSpec as P

BINS = 256
LOG2E = 1.4426950408889634
KAPPA = 0.7 / 0.3
UNROLL = 16
ANY = pl.BlockSpec(memory_space=pl.ANY)
VMEM = pl.BlockSpec(memory_space=pltpu.VMEM)
SMEM = pl.BlockSpec(memory_space=pltpu.SMEM)


def neighbour(array, axis, step):
    size = lax.axis_size(axis)
    pairs = [(i, i + step) for i in range(size) if 0 <= i + step < size]
    return lax.ppermute(array, axis, pairs)


def shifted(array, axis, step):
    size = lax.axis_size(axis)
    return lax.ppermute(array, axis, [(i, (i + step) % size) for i in range(size)])


def columns_kernel(top_ref, bottom_ref, first_ref, last_ref):
    depth = top_ref.shape[0]
    lane = lax.broadcasted_iota(jnp.int32, (8, 128), 1)
    left_half = lane < 64

    def tile(index, _):
        rows = pl.ds(pl.multiple_of(index * 8, 8), 8)
        first = jnp.zeros((8, 128), jnp.float32)
        last = jnp.zeros((8, 128), jnp.float32)
        for half, ref in enumerate((top_ref, bottom_ref)):
            for z in range(depth):
                place = half * 64 + z
                ends = jnp.where(left_half, ref[z, rows, 0:128], ref[z, rows, 128:256])
                moved = ends if place == 0 else pltpu.roll(ends, place, 1)
                first = jnp.where(lane == place, moved, first)
                last = jnp.where(lane == (place - 1) % 128, moved, last)
        first_ref[rows, :] = first
        last_ref[rows, :] = pltpu.roll(last, 1, 1)
        return 0

    lax.fori_loop(0, first_ref.shape[0] // 8, tile, 0)


def columns(density):
    depth, rows, cols = density.shape
    half, block = rows // 2, 16
    steps = half // block
    return pl.pallas_call(
        columns_kernel,
        name="columns",
        grid=(steps,),
        out_shape=[jax.ShapeDtypeStruct((half, 128), jnp.float32)] * 2,
        in_specs=[
            pl.BlockSpec((depth, block, cols), lambda i: (0, i, 0)),
            pl.BlockSpec((depth, block, cols), lambda i: (0, i + steps, 0)),
        ],
        out_specs=[pl.BlockSpec((block, 128), lambda i: (i, 0))] * 2,
        compiler_params=pltpu.CompilerParams(vmem_limit_bytes=16 * 2**20),
        cost_estimate=pl.CostEstimate(flops=10**7, bytes_accessed=density.size * 4, transcendentals=0),
    )(density, density)


def march_kernel(
    shift, groups, rank_ref, knots_ref, color_ref, sigma_ref, x_hbm, zlo_hbm, zhi_hbm, ylo_ref, yhi_ref,
    xlo_hbm, xhi_hbm, out_ref, buf, lo_buf, hi_buf, sems, side_sems,
):
    depth, total_rows, _ = x_hbm.shape
    rows = out_ref.shape[1]
    tiles = rows // 8
    half = total_rows // 2
    mine = lax.axis_index("gz")
    piece = lax.rem(mine + shift, groups)
    y0 = pl.multiple_of(piece * rows, rows)
    forward = rank_ref[0] < rank_ref[groups - 1]
    is_first = piece == 0
    is_last = piece == groups - 1
    inv_depth = 1.0 / (depth * groups)

    def chunk(t, c):
        return pltpu.make_async_copy(
            x_hbm.at[:, pl.ds(pl.multiple_of(y0 + 8 * t, 8), 8), pl.ds(128 * c, 128)],
            buf.at[c, pl.ds(1, depth), pl.ds(pl.multiple_of(8 * (t + 1), 8), 8), :],
            sems.at[t + 1, c],
        )

    def face(c, end):
        return pltpu.make_async_copy(
            (zhi_hbm if end else zlo_hbm).at[pl.ds(y0, rows), pl.ds(128 * c, 128)],
            buf.at[c, (depth + 1) * end, pl.ds(8, rows), :],
            side_sems.at[end, c],
        )

    fold = pl.multiple_of(lax.rem(y0, half), rows)
    folded = jnp.where(y0 >= half, 64, 0)
    sides = [
        pltpu.make_async_copy(xlo_hbm.at[pl.ds(fold, rows), :], lo_buf, side_sems.at[2, 0]),
        pltpu.make_async_copy(xhi_hbm.at[pl.ds(fold, rows), :], hi_buf, side_sems.at[2, 1]),
    ] + [face(c, end) for c in range(2) for end in range(2)]
    for copy in sides:
        copy.start()

    @pl.when(jnp.logical_not(is_first))
    def _():
        for c in range(2):
            chunk(-1, c).start()

    for t in range(tiles):
        for c in range(2):
            chunk(t, c).start()

    @pl.when(jnp.logical_not(is_last))
    def _():
        for c in range(2):
            chunk(tiles, c).start()

    def put_row(ref, row):
        def body(group, _):
            for c in range(2):
                value = ref[pl.ds(pl.multiple_of(group * 8, 8), 8), pl.ds(128 * c, 128)]
                for k in range(8):
                    buf[c, 1 + group * 8 + k, pl.ds(row, 1), :] = value[k : k + 1, :]
            return 0

        lax.fori_loop(0, depth // 8, body, 0)

    @pl.when(is_first)
    def _():
        put_row(ylo_ref, 7)

    @pl.when(is_last)
    def _():
        put_row(yhi_ref, 8 + rows)

    def full(value):
        return jnp.full((8, 128), value, jnp.float32)

    knot = [knots_ref[k].astype(jnp.float32) * (1.0 / (BINS - 1.0)) for k in range(8)]
    widths = [full(knot[k + 1] - knot[k]) for k in range(7)]
    inverse = [1.0 / width for width in widths]
    scale = -LOG2E * inv_depth
    slopes = [full((sigma_ref[k + 1] - sigma_ref[k]) * scale) * inverse[k] for k in range(7)]
    base = full(sigma_ref[0] * scale)
    sign = jnp.where(forward, 1.0, -1.0)
    light_z = full(sign * (0.64 * KAPPA))
    offset = jnp.where(forward, mine, groups - 1 - mine) * depth
    depth_0 = (offset.astype(jnp.float32) + 0.5) * inv_depth
    step = jnp.where(forward, 1, -1)
    start = jnp.where(forward, 1, depth)
    lane = lax.broadcasted_iota(jnp.int32, (8, 128), 1)
    at_first = lane == 0
    at_last = lane == 127

    for copy in sides:
        copy.wait()

    @pl.when(jnp.logical_not(is_first))
    def _():
        for c in range(2):
            chunk(-1, c).wait()

    for c in range(2):
        chunk(0, c).wait()

    def tile(t, _):
        @pl.when(jnp.logical_or(t < tiles - 1, jnp.logical_not(is_last)))
        def _():
            for c in range(2):
                chunk(t + 1, c).wait()

        r = pl.multiple_of(8 * t + 8, 8)
        out_rows = pl.ds(pl.multiple_of(8 * t, 8), 8)
        side_lo = lo_buf[out_rows, :]
        side_hi = hi_buf[out_rows, :]
        zero = full(0.0)
        state = ((full(1.0),) + (zero,) * 12,) * 2
        before = tuple(buf[c, start - step, pl.ds(r, 8), :] for c in range(2))
        here = tuple(buf[c, start, pl.ds(r, 8), :] for c in range(2))

        def gradient_x(left, right, z):
            place = z - 1 + folded
            lo = pltpu.roll(side_lo, 128 - place, 1)
            hi = pltpu.roll(side_hi, 127 - place, 1)
            left_next, left_prev = pltpu.roll(left, 127, 1), pltpu.roll(left, 1, 1)
            right_next, right_prev = pltpu.roll(right, 127, 1), pltpu.roll(right, 1, 1)
            return (
                jnp.where(at_last, right_next, left_next) - jnp.where(at_first, lo, left_prev),
                jnp.where(at_last, hi, right_next) - jnp.where(at_first, left_prev, right_prev),
            )

        def block(b, carry):
            before, here, state = carry
            state = [list(s) for s in state]
            for k in range(UNROLL):
                z = start + step * (b * UNROLL + k)
                after = tuple(buf[c, z + step, pl.ds(r, 8), :] for c in range(2))
                grad_x = gradient_x(here[0], here[1], z)
                for c in range(2):
                    s = state[c]
                    gx = grad_x[c]
                    gy = buf[c, z, pl.ds(r + 1, 8), :] - buf[c, z, pl.ds(r - 1, 8), :]
                    gz = after[c] - before[c]
                    factor = lax.rsqrt(jnp.maximum(gx * gx + gy * gy + gz * gz, 0.25))
                    light = gx * (0.48 * KAPPA) + gy * (0.6 * KAPPA) + gz * light_z
                    rest = here[c]
                    ramps = []
                    power = base
                    for j in range(7):
                        ramp = jnp.minimum(rest, widths[j]) if j < 6 else rest
                        rest = rest - ramp
                        ramps.append(ramp)
                        power = power + ramp * slopes[j]
                    clear = s[0] * jnp.exp2(power)
                    weight = s[0] - clear
                    scaled = weight * factor
                    shaded = weight + scaled * jnp.abs(light)
                    s[1] = s[1] + s[0]
                    s[0] = clear
                    s[2] = s[2] + shaded
                    for j in range(7):
                        s[3 + j] = s[3 + j] + shaded * ramps[j]
                    s[10] = s[10] + scaled * gx
                    s[11] = s[11] + scaled * gy
                    s[12] = s[12] + scaled * gz
                before, here = here, after
            return before, here, tuple(tuple(s) for s in state)

        _, _, state = lax.fori_loop(0, depth // UNROLL, block, (before, here, state))
        for c in range(2):
            s = state[c]
            cols = pl.ds(128 * c, 128)
            for channel in range(3):
                total = s[2] * (color_ref[channel, 0] * 0.3)
                for j in range(7):
                    rise = (color_ref[channel, j + 1] - color_ref[channel, j]) * 0.3
                    total = total + s[3 + j] * (inverse[j] * rise)
                out_ref[channel, out_rows, cols] = total
            opacity = 1.0 - s[0]
            out_ref[3, out_rows, cols] = opacity
            out_ref[4, out_rows, cols] = opacity * depth_0 + (s[1] - 1.0 - s[0] * (depth - 1.0)) * inv_depth
            out_ref[5, out_rows, cols] = s[10]
            out_ref[6, out_rows, cols] = s[11]
            out_ref[7, out_rows, cols] = s[12] * sign
        return 0

    lax.fori_loop(0, tiles, tile, 0)


def march(shift, groups, tables, density, sides):
    depth, total_rows, cols = density.shape
    rows = total_rows // groups
    voxels = depth * rows * cols

    def kernel(*refs):
        march_kernel(shift, groups, *refs)

    return pl.pallas_call(
        kernel,
        name="march",
        out_shape=jax.ShapeDtypeStruct((8, rows, cols), jnp.float32),
        in_specs=[SMEM] * 4 + [ANY] * 3 + [VMEM] * 2 + [ANY] * 2,
        out_specs=VMEM,
        scratch_shapes=[
            pltpu.VMEM((2, depth + 2, rows + 16, 128), jnp.float32),
            pltpu.VMEM((rows, 128), jnp.float32),
            pltpu.VMEM((rows, 128), jnp.float32),
            pltpu.SemaphoreType.DMA((rows // 8 + 2, 2)),
            pltpu.SemaphoreType.DMA((3, 2)),
        ],
        compiler_params=pltpu.CompilerParams(vmem_limit_bytes=24 * 2**20),
        cost_estimate=pl.CostEstimate(flops=72 * voxels, bytes_accessed=voxels * 4, transcendentals=2 * voxels),
    )(*tables, density, *sides)


def body(density, depth_rank, knots, tf_color, tf_sigma):
    depth, rows, cols = density.shape
    groups = lax.axis_size("gz")
    zlo = neighbour(density[depth - 1], "gz", 1)
    zhi = neighbour(density[0], "gz", -1)
    ylo = neighbour(density[:, rows - 1, :], "gy", 1)
    yhi = neighbour(density[:, 0, :], "gy", -1)
    first, last = columns(density)
    xlo = neighbour(last, "gx", 1)
    xhi = neighbour(first, "gx", -1)
    tables = (depth_rank, knots, tf_color, tf_sigma)
    sides = (zlo, zhi, ylo, yhi, xlo, xhi)
    parts = [None] * groups
    for shift in (2, 1, 3, 0):
        piece = march(shift, groups, tables, density, sides)
        parts[shift] = piece if shift == 0 else shifted(piece, "gz", shift)
    mine = lax.axis_index("gz")
    forward = depth_rank[0] < depth_rank[groups - 1]
    slabs = [lax.rem(mine - s + groups, groups) for s in range(groups)]
    image = 0.0
    for s in range(groups):
        seen = parts[s]
        for other in range(groups):
            if other != s:
                nearer = (slabs[other] < slabs[s]) == forward
                seen = seen * jnp.where(nearer, 1.0 - parts[other][3:4], 1.0)
        image = image + seen
    return image


def solution(mesh):
    in_specs = (P("gz", "gy", "gx"), P(), P(), P(), P())
    out_specs = P(None, ("gy", "gz"), "gx")
    return jax.shard_map(body, mesh=mesh, in_specs=in_specs, out_specs=out_specs, check_vma=False)
```

time: 744 us -> 104 us (0.14)
  other arithmetic: 621 us -> 1.18 us
  Pallas kernels: 0 us -> 58.4 us
  waiting for transfers between devices: 35.6 us -> 4.14 us
  local copies, waits for them, and re-layouts: 44.8 us -> 14.5 us
  between operations: 15.2 us -> 1.55 us
    reduce_sum x16 -> x0, other arithmetic: 470 us -> none  [the longest x4 154 us: march(): jnp.sum(weight * feats[5], axis=0)]
    another operation x4 -> x0, other arithmetic: 110 us -> none  [march(): running = jnp.cumsum(tau, axis=0)]
    pallas_call x0 -> x5, Pallas kernels: none -> 58.4 us  [the longest x4 52.9 us: march(): pl.pallas_call(kernel, name='march', out_shape=jax.ShapeDtypeStruct((8, r...]
    ppermute x8 -> x9, waiting for transfers between devices: 35.6 us -> 4.14 us  [the longest x6 4.14 us: neighbour(): return lax.ppermute(array, axis, pairs)]
    concatenate x1 -> x0, other arithmetic: 26.9 us -> none  [padded_2(): array = jnp.concatenate([before, array, after], axis=dim)]
    slice x14 -> x2, local copies, waits for them, and re-layouts: 19.9 us -> 1.88 us  [the longest x1 1.3 us: body(): yhi = neighbour(density[:, 0, :], 'gy', -1)]
    ppermute x2 -> x0, local copies, waits for them, and re-layouts: 9.32 us -> none  [the longest x1 4.68 us: padded_2(): after = lax.ppermute(leading, axis, down)]
    ppermute x8 -> x9, starting transfers between devices: 22.7 us -> 23.7 us  [the longest x6 16.1 us: neighbour(): return lax.ppermute(array, axis, pairs)]
  transfers between devices with their start and end apart: 8 -> 9, of which waited for: 4 -> 2; matrix products, arithmetic and copies ran while one was open for 2% -> 2% of each run, Pallas kernels for 0% -> 44%
where the time goes in v1:
time: 104 us; the launch traced here: 103 us
  Pallas kernels  58.4 us (56%)
  starting transfers between devices  23.7 us (23%)
  local copies, waits for them, and re-layouts  14.5 us (14%)
  waiting for transfers between devices  4.14 us (4%)
  between operations  1.55 us (1%)
  other arithmetic  1.18 us (1%)
    pallas_call x4, Pallas kernels, march(): pl.pallas_call(kernel, name='march', out_shape=jax.ShapeDtypeStruct((8, r...  52.9 us
    ppermute x6, starting transfers between devices, neighbour(): return lax.ppermute(array, axis, pairs)  16.1 us
    unnamed x16, local copies, waits for them, and re-layouts  11.6 us
    ppermute x3, starting transfers between devices, shifted(): lax.ppermute(array, axis, [(i, (i + step) % size) for i in range(size)])  7.61 us
    pallas_call x1, Pallas kernels, columns(): pl.pallas_call(columns_kernel, name='columns', grid=(steps,), out_shape=[...  5.5 us
    ppermute x6, waiting for transfers between devices, neighbour(): return lax.ppermute(array, axis, pairs)  4.14 us
  transfers between devices with their start and end apart: 9, of which 2 were waited for; matrix products, arithmetic and copies ran while one was open for 2% of the time, Pallas kernels for 44%

profile of v1, /device:TPU:40, one launch (start us, length us, event | category | flops | bytes accessed | tf_op | source)
XLA Modules:
  0.0 103.5 jit_solution(13437452573461884329)
XLA Ops:
  0.0 1.1 %slice_bitcast_fusion = (f32[256,256]{1,0:T(8,128)S(1)}, f32[256,256]{1,0:T(8,128)S(1)}) fusion(f32[64,256,256]{2,1,0:T(8,128)} %refs_4_.7), kind=kLoop, calls=%fused_computation.1 | loop fusion | bytes 1048576 | tf_op jit(solution)/shard_map/squeeze | solution.py:285
  1.1 3.4 %collective-permute-start = (f32[256,256]{1,0:T(8,128)S(1)}, f32[256,256]{1,0:T(8,128)S(1)}, u32[]{:S(2)}, u32[]{:S(2)}) collective-permute-start(f32[256,256]{1,0:T(8,128)S(1)} %get-tuple-element.12), channel_id=1, source_target_pairs={{0,1},{1,2},{2,3},{4,5},{5,6},{6,7},{8,9},{9,10},{10,11},{12,13},{... | collective-permute-start | bytes 786440 | tf_op jit(solution)/shard_map/ppermute | solution.py:20
  4.5 1.3 %collective-permute-start.1 = (f32[256,256]{1,0:T(8,128)S(1)}, f32[256,256]{1,0:T(8,128)S(1)}, u32[]{:S(2)}, u32[]{:S(2)}) collective-permute-start(f32[256,256]{1,0:T(8,128)S(1)} %get-tuple-element.11), channel_id=1, source_target_pairs={{1,0},{2,1},{3,2},{5,4},{6,5},{7,6},{9,8},{10,9},{11,10},{13,12},{... | collective-permute-start | bytes 786440 | tf_op jit(solution)/shard_map/ppermute | solution.py:20
  5.8 1.3 %fusion = (f32[64,1,256]{2,1,0:T(1,128)S(1)}, f32[64,1,256]{2,1,0:T(1,128)S(1)}) fusion(f32[64,256,256]{2,1,0:T(8,128)} %refs_4_.7), kind=kLoop, calls=%fused_computation.21 | loop fusion | bytes 262144 | tf_op jit(solution)/shard_map/slice | solution.py:287
  7.1 1.9 %collective-permute-start.2 = (f32[64,256]{1,0:T(8,128)S(1)}, f32[64,256]{1,0:T(8,128)S(1)}, u32[]{:S(2)}, u32[]{:S(2)}) collective-permute-start(f32[64,256]{1,0:T(8,128)S(1)} %bitcast.36), channel_id=1, source_target_pairs={{0,4},{4,8},{8,12},{12,16},{16,20},{20,24},{24,28},{1,5},{5,9},{9,... | collective-permute-start | bytes 196616 | tf_op jit(solution)/shard_map/ppermute | solution.py:20
  9.0 3.6 %collective-permute-start.3 = (f32[64,256]{1,0:T(8,128)S(1)}, f32[64,256]{1,0:T(8,128)S(1)}, u32[]{:S(2)}, u32[]{:S(2)}) collective-permute-start(f32[64,256]{1,0:T(8,128)S(1)} %bitcast.35), channel_id=1, source_target_pairs={{4,0},{8,4},{12,8},{16,12},{20,16},{24,20},{28,24},{5,1},{9,5},{13... | collective-permute-start | bytes 196616 | tf_op jit(solution)/shard_map/ppermute | solution.py:20
  12.7 5.8 %copy-done = f32[64,256,256]{2,1,0:T(8,128)S(1)} copy-done((f32[64,256,256]{2,1,0:T(8,128)S(1)}, f32[64,256,256]{2,1,0:T(8,128)}, u32[]{:S(2)}) %copy-start) | copy-done | bytes 16777240
  18.5 0.0 copy-start.6
  18.5 5.5 %columns.1 = (f32[128,128]{1,0:T(8,128)S(1)}, f32[128,128]{1,0:T(8,128)S(1)}) custom-call(f32[64,256,256]{2,1,0:T(8,128)S(1)} %copy-done, f32[64,256,256]{2,1,0:T(8,128)S(1)} %copy-done), custom_call_target="tpu_custom_call" | custom-call | flops 10000000 | bytes 16777216 | tf_op jit(solution)/shard_map/columns/pallas_call | solution.py:55
  24.0 3.8 %collective-permute-start.4 = (f32[128,128]{1,0:T(8,128)S(1)}, f32[128,128]{1,0:T(8,128)S(1)}, u32[]{:S(2)}, u32[]{:S(2)}) collective-permute-start(f32[128,128]{1,0:T(8,128)S(1)} %get-tuple-element.7), channel_id=1, source_target_pairs={{0,32},{32,64},{64,96},{1,33},{33,65},{65,97},{2,34},{34,66},{66,9... | collective-permute-start | bytes 196616 | tf_op jit(solution)/shard_map/ppermute | solution.py:20
  27.8 2.0 %collective-permute-start.5 = (f32[128,128]{1,0:T(8,128)S(1)}, f32[128,128]{1,0:T(8,128)S(1)}, u32[]{:S(2)}, u32[]{:S(2)}) collective-permute-start(f32[128,128]{1,0:T(8,128)S(1)} %get-tuple-element.8), channel_id=1, source_target_pairs={{32,0},{64,32},{96,64},{33,1},{65,33},{97,65},{34,2},{66,34},{98,6... | collective-permute-start | bytes 196616 | tf_op jit(solution)/shard_map/ppermute | solution.py:20
  29.9 0.3 collective-permute-done.4.refs_9_
  30.1 3.8 %collective-permute-done.5.refs_10_ = f32[128,128]{1,0:T(8,128)S(1)} collective-permute-done((f32[128,128]{1,0:T(8,128)S(1)}, f32[128,128]{1,0:T(8,128)S(1)}, u32[]{:S(2)}, u32[]{:S(2)}) %collective-permute-start.5) | collective-permute-done | bytes 65568 | tf_op jit(solution)/shard_map/ppermute | solution.py:20
  34.0 13.2 %march.6 = f32[8,64,256]{2,1,0:T(8,128)S(1)} custom-call(s32[4]{0:T(128)S(1)} %copy-done.4, s32[8]{0:T(128)S(1)} %copy-done.5, f32[3,8]{1,0:T(4,128)S(1)} %copy-done.3, f32[8]{0:T(128)S(1)} %copy-done.6, f32[64,256,256]{2,1,0:T(8,128)S(1)} %copy-done.1, f32[256,256]{1,0:T(8,128)S(1)} %collective-permute-done.refs_5_, ...), custom_call_target="tpu_custom_call" | custom-call | flops 75497472 | bytes 4194304 | tf_op jit(solution)/shard_map/march/pallas_call | solution.py:263
  47.3 4.2 %collective-permute-start.7 = (f32[8,64,256]{2,1,0:T(8,128)S(1)}, f32[8,64,256]{2,1,0:T(8,128)S(1)}, u32[]{:S(2)}, u32[]{:S(2)}) collective-permute-start(f32[8,64,256]{2,1,0:T(8,128)S(1)} %march.6), channel_id=1, source_target_pairs={{0,2},{1,3},{2,0},{3,1},{4,6},{5,7},{6,4},{7,5},{8,10},{9,11},{10,... | collective-permute-start | bytes 1572872 | tf_op jit(solution)/shard_map/ppermute | solution.py:25
  51.5 13.2 %march.5 = f32[8,64,256]{2,1,0:T(8,128)S(1)} custom-call(s32[4]{0:T(128)S(1)} %copy-done.4, s32[8]{0:T(128)S(1)} %copy-done.5, f32[3,8]{1,0:T(4,128)S(1)} %copy-done.3, f32[8]{0:T(128)S(1)} %copy-done.6, f32[64,256,256]{2,1,0:T(8,128)S(1)} %copy-done.1, f32[256,256]{1,0:T(8,128)S(1)} %collective-permute-done.refs_5_, ...), custom_call_target="tpu_custom_call" | custom-call | flops 75497472 | bytes 4194304 | tf_op jit(solution)/shard_map/march/pallas_call | solution.py:263
  64.7 0.7 collective-permute-start.6
  65.4 0.6 fusion.1
  67.3 0.0 copy-start.2
  67.3 5.8 %copy-done.2 = f32[64,256,256]{2,1,0:T(8,128)S(1)} copy-done((f32[64,256,256]{2,1,0:T(8,128)S(1)}, f32[64,256,256]{2,1,0:T(8,128)}, u32[]{:S(2)}) %copy-start.2) | copy-done | bytes 16777240
  73.1 13.2 %march.7 = f32[8,64,256]{2,1,0:T(8,128)S(1)} custom-call(s32[4]{0:T(128)S(1)} %copy-done.4, s32[8]{0:T(128)S(1)} %copy-done.5, f32[3,8]{1,0:T(4,128)S(1)} %copy-done.3, f32[8]{0:T(128)S(1)} %copy-done.6, f32[64,256,256]{2,1,0:T(8,128)S(1)} %copy-done.2, f32[256,256]{1,0:T(8,128)S(1)} %collective-permute-done.refs_5_, ...), custom_call_target="tpu_custom_call" | custom-call | flops 75497472 | bytes 4194304 | tf_op jit(solution)/shard_map/march/pallas_call | solution.py:263
  86.3 2.7 %collective-permute-start.8 = (f32[8,64,256]{2,1,0:T(8,128)S(1)}, f32[8,64,256]{2,1,0:T(8,128)S(1)}, u32[]{:S(2)}, u32[]{:S(2)}) collective-permute-start(f32[8,64,256]{2,1,0:T(8,128)S(1)} %march.7), channel_id=1, source_target_pairs={{0,3},{1,0},{2,1},{3,2},{4,7},{5,4},{6,5},{7,6},{8,11},{9,8},{10,9... | collective-permute-start | bytes 1572872 | tf_op jit(solution)/shard_map/ppermute | solution.py:25
  89.0 13.2 %march.4 = f32[8,64,256]{2,1,0:T(8,128)S(1)} custom-call(s32[4]{0:T(128)S(1)} %copy-done.4, s32[8]{0:T(128)S(1)} %copy-done.5, f32[3,8]{1,0:T(4,128)S(1)} %copy-done.3, f32[8]{0:T(128)S(1)} %copy-done.6, f32[64,256,256]{2,1,0:T(8,128)S(1)} %copy-done.2, f32[256,256]{1,0:T(8,128)S(1)} %collective-permute-done.refs_5_, ...), custom_call_target="tpu_custom_call" | custom-call | flops 75497472 | bytes 4194304 | tf_op jit(solution)/shard_map/march/pallas_call | solution.py:263
  102.4 1.1 %multiply_add_fusion = f32[8,64,256]{2,1,0:T(8,128)} fusion(f32[8,64,256]{2,1,0:T(8,128)S(1)} %collective-permute-done.8, f32[8,64,256]{2,1,0:T(8,128)S(1)} %collective-permute-done.7, f32[8,64,256]{2,1,0:T(8,128)S(1)} %collective-permute-done.6, f32[8,64,256]{2,1,0:T(8,128)S(1)} %march.4, f32[64,256]{1,0:T(8,128)S(1)} %get-tuple-element.18, ...), kind=kLoop, calls=%fused_computation | loop fusion | flops 1966080 | bytes 3407872 | tf_op jit(solution)/shard_map/add | solution.py:307
  (23 shorter events, 0.1 us)
Async XLA Ops:
  1.1 32.9 %collective-permute-start = (f32[256,256]{1,0:T(8,128)S(1)}, f32[256,256]{1,0:T(8,128)S(1)}, u32[]{:S(2)}, u32[]{:S(2)}) collective-permute-start(f32[256,256]{1,0:T(8,128)S(1)} %get-tuple-element.12), channel_id=1, source_target_pairs={{0,1},{1,2},{2,3},{4,5},{5,6},{6,7},{8,9},{9,10},{10,11},{12,13},{... | collective-permute-start | bytes 786440 | tf_op jit(solution)/shard_map/ppermute | solution.py:20
  4.5 29.5 %collective-permute-start.1 = (f32[256,256]{1,0:T(8,128)S(1)}, f32[256,256]{1,0:T(8,128)S(1)}, u32[]{:S(2)}, u32[]{:S(2)}) collective-permute-start(f32[256,256]{1,0:T(8,128)S(1)} %get-tuple-element.11), channel_id=1, source_target_pairs={{1,0},{2,1},{3,2},{5,4},{6,5},{7,6},{9,8},{10,9},{11,10},{13,12},{... | collective-permute-start | bytes 786440 | tf_op jit(solution)/shard_map/ppermute | solution.py:20
  7.1 20.7 %collective-permute-start.2 = (f32[64,256]{1,0:T(8,128)S(1)}, f32[64,256]{1,0:T(8,128)S(1)}, u32[]{:S(2)}, u32[]{:S(2)}) collective-permute-start(f32[64,256]{1,0:T(8,128)S(1)} %bitcast.36), channel_id=1, source_target_pairs={{0,4},{4,8},{8,12},{12,16},{16,20},{20,24},{24,28},{1,5},{5,9},{9,... | collective-permute-start | bytes 196616 | tf_op jit(solution)/shard_map/ppermute | solution.py:20
  9.0 20.8 %collective-permute-start.3 = (f32[64,256]{1,0:T(8,128)S(1)}, f32[64,256]{1,0:T(8,128)S(1)}, u32[]{:S(2)}, u32[]{:S(2)}) collective-permute-start(f32[64,256]{1,0:T(8,128)S(1)} %bitcast.35), channel_id=1, source_target_pairs={{4,0},{8,4},{12,8},{16,12},{20,16},{24,20},{28,24},{5,1},{9,5},{13... | collective-permute-start | bytes 196616 | tf_op jit(solution)/shard_map/ppermute | solution.py:20
  12.7 5.8 %copy-start = (f32[64,256,256]{2,1,0:T(8,128)S(1)}, f32[64,256,256]{2,1,0:T(8,128)}, u32[]{:S(2)}) copy-start(f32[64,256,256]{2,1,0:T(8,128)} %refs_4_.7) | copy-start | bytes 50331652
  18.5 15.5 %copy-start.1 = (f32[64,256,256]{2,1,0:T(8,128)S(1)}, f32[64,256,256]{2,1,0:T(8,128)}, u32[]{:S(2)}) copy-start(f32[64,256,256]{2,1,0:T(8,128)} %refs_4_.7) | copy-start | bytes 50331652
  18.5 15.5 %copy-start.3 = (f32[3,8]{1,0:T(4,128)S(1)}, f32[3,8]{1,0:T(4,128)}, u32[]{:S(2)}) copy-start(f32[3,8]{1,0:T(4,128)} %refs_2_.7) | copy-start | bytes 292
  18.5 15.5 %copy-start.4 = (s32[4]{0:T(128)S(1)}, s32[4]{0:T(128)}, u32[]{:S(2)}) copy-start(s32[4]{0:T(128)} %refs_0_.7) | copy-start | bytes 52
  18.5 15.5 %copy-start.5 = (s32[8]{0:T(128)S(1)}, s32[8]{0:T(128)}, u32[]{:S(2)}) copy-start(s32[8]{0:T(128)} %refs_1_.7) | copy-start | bytes 100
  18.5 15.6 %copy-start.6 = (f32[8]{0:T(128)S(1)}, f32[8]{0:T(128)}, u32[]{:S(2)}) copy-start(f32[8]{0:T(128)} %refs_3_.7) | copy-start | bytes 100
  24.0 6.2 %collective-permute-start.4 = (f32[128,128]{1,0:T(8,128)S(1)}, f32[128,128]{1,0:T(8,128)S(1)}, u32[]{:S(2)}, u32[]{:S(2)}) collective-permute-start(f32[128,128]{1,0:T(8,128)S(1)} %get-tuple-element.7), channel_id=1, source_target_pairs={{0,32},{32,64},{64,96},{1,33},{33,65},{65,97},{2,34},{34,66},{66,9... | collective-permute-start | bytes 196616 | tf_op jit(solution)/shard_map/ppermute | solution.py:20
  27.8 6.2 %collective-permute-start.5 = (f32[128,128]{1,0:T(8,128)S(1)}, f32[128,128]{1,0:T(8,128)S(1)}, u32[]{:S(2)}, u32[]{:S(2)}) collective-permute-start(f32[128,128]{1,0:T(8,128)S(1)} %get-tuple-element.8), channel_id=1, source_target_pairs={{32,0},{64,32},{96,64},{33,1},{65,33},{97,65},{34,2},{66,34},{98,6... | collective-permute-start | bytes 196616 | tf_op jit(solution)/shard_map/ppermute | solution.py:20
  47.3 55.0 %collective-permute-start.7 = (f32[8,64,256]{2,1,0:T(8,128)S(1)}, f32[8,64,256]{2,1,0:T(8,128)S(1)}, u32[]{:S(2)}, u32[]{:S(2)}) collective-permute-start(f32[8,64,256]{2,1,0:T(8,128)S(1)} %march.6), channel_id=1, source_target_pairs={{0,2},{1,3},{2,0},{3,1},{4,6},{5,7},{6,4},{7,5},{8,10},{9,11},{10,... | collective-permute-start | bytes 1572872 | tf_op jit(solution)/shard_map/ppermute | solution.py:25
  64.7 37.6 %collective-permute-start.6 = (f32[8,64,256]{2,1,0:T(8,128)S(1)}, f32[8,64,256]{2,1,0:T(8,128)S(1)}, u32[]{:S(2)}, u32[]{:S(2)}) collective-permute-start(f32[8,64,256]{2,1,0:T(8,128)S(1)} %march.5), channel_id=1, source_target_pairs={{0,1},{1,2},{2,3},{3,0},{4,5},{5,6},{6,7},{7,4},{8,9},{9,10},{10,1... | collective-permute-start | bytes 1572872 | tf_op jit(solution)/shard_map/ppermute | solution.py:25
  67.3 5.8 %copy-start.2 = (f32[64,256,256]{2,1,0:T(8,128)S(1)}, f32[64,256,256]{2,1,0:T(8,128)}, u32[]{:S(2)}) copy-start(f32[64,256,256]{2,1,0:T(8,128)} %refs_4_.7) | copy-start | bytes 50331652
  86.3 16.0 %collective-permute-start.8 = (f32[8,64,256]{2,1,0:T(8,128)S(1)}, f32[8,64,256]{2,1,0:T(8,128)S(1)}, u32[]{:S(2)}, u32[]{:S(2)}) collective-permute-start(f32[8,64,256]{2,1,0:T(8,128)S(1)} %march.7), channel_id=1, source_target_pairs={{0,3},{1,0},{2,1},{3,2},{4,7},{5,4},{6,5},{7,6},{8,11},{9,8},{10,9... | collective-permute-start | bytes 1572872 | tf_op jit(solution)/shard_map/ppermute | solution.py:25

commit v2 on v1

--- a/solution.py
+++ b/solution.py
@@ -8,7 +8,10 @@
 BINS = 256
 LOG2E = 1.4426950408889634
 KAPPA = 0.7 / 0.3
-UNROLL = 16
+UNROLL = 64
+SPLIT = 4
+AHEAD = 5
+ROOM = 50 * 2**20
 ANY = pl.BlockSpec(memory_space=pl.ANY)
 VMEM = pl.BlockSpec(memory_space=pltpu.VMEM)
 SMEM = pl.BlockSpec(memory_space=pltpu.SMEM)
@@ -25,46 +28,69 @@
     return lax.ppermute(array, axis, [(i, (i + step) % size) for i in range(size)])
 
 
-def columns_kernel(top_ref, bottom_ref, first_ref, last_ref):
-    depth = top_ref.shape[0]
+def layers_kernel(x_hbm, x_first, x_last, y_first, y_last, z_first, z_last, buf, sems, z_sems):
+    depth, rows, _ = x_hbm.shape
+    tiles = rows // 8
+    planes = [
+        pltpu.make_async_copy(x_hbm.at[0], z_first, z_sems.at[0]),
+        pltpu.make_async_copy(x_hbm.at[depth - 1], z_last, z_sems.at[1]),
+    ]
+
+    def chunk(t):
+        at = pl.ds(pl.multiple_of(8 * t, 8), 8)
+        return pltpu.make_async_copy(x_hbm.at[:, at, :], buf.at[:, at, :], sems.at[t])
+
+    for t in range(tiles // 2):
+        chunk(t).start()
+        chunk(t + tiles // 2).start()
+    for plane in planes:
+        plane.start()
     lane = lax.broadcasted_iota(jnp.int32, (8, 128), 1)
     left_half = lane < 64
 
-    def tile(index, _):
-        rows = pl.ds(pl.multiple_of(index * 8, 8), 8)
+    def tile(t, _):
         first = jnp.zeros((8, 128), jnp.float32)
         last = jnp.zeros((8, 128), jnp.float32)
-        for half, ref in enumerate((top_ref, bottom_ref)):
+        for half in range(2):
+            row_tile = t + half * (tiles // 2)
+            chunk(row_tile).wait()
+            at = pl.ds(pl.multiple_of(8 * row_tile, 8), 8)
             for z in range(depth):
                 place = half * 64 + z
-                ends = jnp.where(left_half, ref[z, rows, 0:128], ref[z, rows, 128:256])
+                ends = jnp.where(left_half, buf[z, at, 0:128], buf[z, at, 128:256])
                 moved = ends if place == 0 else pltpu.roll(ends, place, 1)
                 first = jnp.where(lane == place, moved, first)
                 last = jnp.where(lane == (place - 1) % 128, moved, last)
-        first_ref[rows, :] = first
-        last_ref[rows, :] = pltpu.roll(last, 1, 1)
+        at = pl.ds(pl.multiple_of(8 * t, 8), 8)
+        x_first[at, :] = first
+        x_last[at, :] = pltpu.roll(last, 1, 1)
         return 0
 
-    lax.fori_loop(0, first_ref.shape[0] // 8, tile, 0)
-
-
-def columns(density):
+    lax.fori_loop(0, tiles // 2, tile, 0)
+    for z in range(depth):
+        y_first[pl.ds(z, 1), :] = buf[z, pl.ds(0, 1), :]
+        y_last[pl.ds(z, 1), :] = buf[z, pl.ds(rows - 1, 1), :]
+    for plane in planes:
+        plane.wait()
+
+
+def layers(density):
     depth, rows, cols = density.shape
-    half, block = rows // 2, 16
-    steps = half // block
+    shape = lambda *dims: jax.ShapeDtypeStruct(dims, jnp.float32)
     return pl.pallas_call(
-        columns_kernel,
-        name="columns",
-        grid=(steps,),
-        out_shape=[jax.ShapeDtypeStruct((half, 128), jnp.float32)] * 2,
-        in_specs=[
-            pl.BlockSpec((depth, block, cols), lambda i: (0, i, 0)),
-            pl.BlockSpec((depth, block, cols), lambda i: (0, i + steps, 0)),
+        layers_kernel,
+        name="layers",
+        out_shape=[shape(rows // 2, 128)] * 2 + [shape(depth, cols)] * 2 + [shape(rows, cols)] * 2,
+        in_specs=[ANY],
+        out_specs=[VMEM] * 4 + [ANY] * 2,
+        scratch_shapes=[
+            pltpu.VMEM(density.shape, jnp.float32),
+            pltpu.SemaphoreType.DMA((rows // 8,)),
+            pltpu.SemaphoreType.DMA((2,)),
         ],
-        out_specs=[pl.BlockSpec((block, 128), lambda i: (i, 0))] * 2,
-        compiler_params=pltpu.CompilerParams(vmem_limit_bytes=16 * 2**20),
+        compiler_params=pltpu.CompilerParams(vmem_limit_bytes=ROOM),
         cost_estimate=pl.CostEstimate(flops=10**7, bytes_accessed=density.size * 4, transcendentals=0),
-    )(density, density)
+    )(density)
 
 
 def march_kernel(
@@ -106,19 +132,22 @@
     for copy in sides:
         copy.start()
 
+    def begin(t, parts):
+        each = depth // parts
+        for k in range(parts):
+            for c in range(2):
+                pltpu.make_async_copy(
+                    x_hbm.at[pl.ds(k * each, each), pl.ds(pl.multiple_of(y0 + 8 * t, 8), 8), pl.ds(128 * c, 128)],
+                    buf.at[c, pl.ds(1 + k * each, each), pl.ds(pl.multiple_of(8 * (t + 1), 8), 8), :],
+                    sems.at[t + 1, c],
+                ).start()
+
     @pl.when(jnp.logical_not(is_first))
     def _():
-        for c in range(2):
-            chunk(-1, c).start()
-
-    for t in range(tiles):
-        for c in range(2):
-            chunk(t, c).start()
-
-    @pl.when(jnp.logical_not(is_last))
-    def _():
-        for c in range(2):
-            chunk(tiles, c).start()
+        begin(-1, SPLIT)
+
+    for t in range(AHEAD):
+        begin(t, SPLIT if t < 2 else 1)
 
     def put_row(ref, row):
         def body(group, _):
@@ -173,6 +202,10 @@
         def _():
             for c in range(2):
                 chunk(t + 1, c).wait()
+
+        @pl.when(jnp.logical_or(t < tiles - AHEAD, jnp.logical_and(t == tiles - AHEAD, jnp.logical_not(is_last))))
+        def _():
+            begin(t + AHEAD, 1)
 
         r = pl.multiple_of(8 * t + 8, 8)
         out_rows = pl.ds(pl.multiple_of(8 * t, 8), 8)
@@ -273,39 +306,74 @@
             pltpu.SemaphoreType.DMA((rows // 8 + 2, 2)),
             pltpu.SemaphoreType.DMA((3, 2)),
         ],
-        compiler_params=pltpu.CompilerParams(vmem_limit_bytes=24 * 2**20),
+        compiler_params=pltpu.CompilerParams(vmem_limit_bytes=ROOM),
         cost_estimate=pl.CostEstimate(flops=72 * voxels, bytes_accessed=voxels * 4, transcendentals=2 * voxels),
     )(*tables, density, *sides)
 
 
+def compose_kernel(groups, rank_ref, *refs):
+    parts, out_ref = refs[:groups], refs[groups]
+    mine = lax.axis_index("gz")
+    forward = rank_ref[0] < rank_ref[groups - 1]
+    place = []
+    for s in range(groups):
+        slab = lax.rem(mine - s + groups, groups)
+        place.append(jnp.where(forward, slab, groups - 1 - slab))
+    nearer = [[jnp.where(place[o] < place[s], 1.0, 0.0) for o in range(groups)] for s in range(groups)]
+
+    def tile(t, _):
+        at = pl.ds(pl.multiple_of(8 * t, 8), 8)
+        opacity = [part[3, at, :] for part in parts]
+        dims = []
+        for s in range(groups):
+            dim = 1.0
+            for o in range(groups):
+                if o != s:
+                    dim = dim * (1.0 - opacity[o] * nearer[s][o])
+            dims.append(dim)
+        for channel in range(8):
+            total = dims[0] * parts[0][channel, at, :]
+            for s in range(1, groups):
+                total = total + dims[s] * parts[s][channel, at, :]
+            out_ref[channel, at, :] = total
+        return 0
+
+    lax.fori_loop(0, out_ref.shape[1] // 8, tile, 0)
+
+
+def compose(rank, parts):
+    groups = len(parts)
+
+    def kernel(*refs):
+        compose_kernel(groups, *refs)
+
+    return pl.pallas_call(
+        kernel,
+        name="compose",
+        out_shape=jax.ShapeDtypeStruct(parts[0].shape, jnp.float32),
+        in_specs=[SMEM] + [VMEM] * groups,
+        out_specs=VMEM,
+        compiler_params=pltpu.CompilerParams(vmem_limit_bytes=32 * 2**20),
+        cost_estimate=pl.CostEstimate(flops=10**6, bytes_accessed=5 * parts[0].size * 4, transcendentals=0),
+    )(rank, *parts)
+
+
 def body(density, depth_rank, knots, tf_color, tf_sigma):
-    depth, rows, cols = density.shape
     groups = lax.axis_size("gz")
-    zlo = neighbour(density[depth - 1], "gz", 1)
-    zhi = neighbour(density[0], "gz", -1)
-    ylo = neighbour(density[:, rows - 1, :], "gy", 1)
-    yhi = neighbour(density[:, 0, :], "gy", -1)
-    first, last = columns(density)
-    xlo = neighbour(last, "gx", 1)
-    xhi = neighbour(first, "gx", -1)
+    x_first, x_last, y_first, y_last, z_first, z_last = layers(density)
+    zlo = neighbour(z_last, "gz", 1)
+    zhi = neighbour(z_first, "gz", -1)
+    xlo = neighbour(x_last, "gx", 1)
+    xhi = neighbour(x_first, "gx", -1)
+    ylo = neighbour(y_last, "gy", 1)
+    yhi = neighbour(y_first, "gy", -1)
     tables = (depth_rank, knots, tf_color, tf_sigma)
     sides = (zlo, zhi, ylo, yhi, xlo, xhi)
     parts = [None] * groups
     for shift in (2, 1, 3, 0):
         piece = march(shift, groups, tables, density, sides)
         parts[shift] = piece if shift == 0 else shifted(piece, "gz", shift)
-    mine = lax.axis_index("gz")
-    forward = depth_rank[0] < depth_rank[groups - 1]
-    slabs = [lax.rem(mine - s + groups, groups) for s in range(groups)]
-    image = 0.0
-    for s in range(groups):
-        seen = parts[s]
-        for other in range(groups):
-            if other != s:
-                nearer = (slabs[other] < slabs[s]) == forward
-                seen = seen * jnp.where(nearer, 1.0 - parts[other][3:4], 1.0)
-        image = image + seen
-    return image
+    return compose(depth_rank, parts)
 
 
 def solution(mesh):

time: 104 us -> 90.1 us (0.87)
  local copies, waits for them, and re-layouts: 14.5 us -> 0.02 us
  Pallas kernels: 58.4 us -> 62.4 us
  between operations: 1.55 us -> 0.17 us
  other arithmetic: 1.18 us -> 0 us
    unnamed x16 -> x8, local copies, waits for them, and re-layouts: 11.6 us -> 0.02 us
    pallas_call x1 -> x2, Pallas kernels: 5.5 us -> 8.48 us  [the longest x1 6.89 us: layers(): pl.pallas_call(layers_kernel, name='layers', out_shape=[shape(rows // 2,...]
    slice x2 -> x0, local copies, waits for them, and re-layouts: 1.88 us -> none  [the longest x1 1.3 us: body(): yhi = neighbour(density[:, 0, :], 'gy', -1)]
    add x1 -> x0, other arithmetic: 1.09 us -> none  [body(): image = image + seen]
    squeeze x1 -> x0, local copies, waits for them, and re-layouts: 1.06 us -> none  [body(): zhi = neighbour(density[0], 'gz', -1)]
  transfers between devices with their start and end apart: 9 -> 9, of which waited for: 2 -> 2; matrix products, arithmetic and copies ran while one was open for 2% -> 0% of each run, Pallas kernels for 44% -> 45%
where the time goes in v2:
time: 90.1 us; the launch traced here: 89.8 us
  Pallas kernels  62.4 us (69%)
  starting transfers between devices  23.1 us (26%)
  waiting for transfers between devices  4.14 us (5%)
    pallas_call x4, Pallas kernels, march(): pl.pallas_call(kernel, name='march', out_shape=jax.ShapeDtypeStruct((8, r...  53.9 us
    ppermute x6, starting transfers between devices, neighbour(): return lax.ppermute(array, axis, pairs)  16.1 us
    ppermute x3, starting transfers between devices, shifted(): lax.ppermute(array, axis, [(i, (i + step) % size) for i in range(size)])  7.01 us
    pallas_call x1, Pallas kernels, layers(): pl.pallas_call(layers_kernel, name='layers', out_shape=[shape(rows // 2,...  6.89 us
    ppermute x6, waiting for transfers between devices, neighbour(): return lax.ppermute(array, axis, pairs)  4.14 us
  transfers between devices with their start and end apart: 9, of which 2 were waited for; matrix products, arithmetic and copies ran while one was open for 0% of the time, Pallas kernels for 45%

profile of v2, /device:TPU:40, one launch (start us, length us, event | category | flops | bytes accessed | tf_op | source)
XLA Modules:
  0.0 89.8 jit_solution(13801922499349665499)
XLA Ops:
  0.0 6.9 %layers.1 = (f32[128,128]{1,0:T(8,128)S(1)}, f32[128,128]{1,0:T(8,128)S(1)}, f32[64,256]{1,0:T(8,128)S(1)}, f32[64,256]{1,0:T(8,128)S(1)}, f32[256,256]{1,0:T(8,128)S(1)}, /*index=5*/f32[256,256]{1,0:T(8,128)S(1)}) custom-call(f32[64,256,256]{2,1,0:T(8,128)} %refs_4_.7), custom_call_target="tpu_custom_call" | custom-call | flops 10000000 | bytes 16777216 | tf_op jit(solution)/shard_map/layers/pallas_call | solution.py:80
  6.9 3.4 %collective-permute-start = (f32[256,256]{1,0:T(8,128)S(1)}, f32[256,256]{1,0:T(8,128)S(1)}, u32[]{:S(2)}, u32[]{:S(2)}) collective-permute-start(f32[256,256]{1,0:T(8,128)S(1)} %get-tuple-element.11), channel_id=1, source_target_pairs={{0,1},{1,2},{2,3},{4,5},{5,6},{6,7},{8,9},{9,10},{10,11},{12,13},{... | collective-permute-start | bytes 786440 | tf_op jit(solution)/shard_map/ppermute | solution.py:23
  10.3 1.3 %collective-permute-start.1 = (f32[256,256]{1,0:T(8,128)S(1)}, f32[256,256]{1,0:T(8,128)S(1)}, u32[]{:S(2)}, u32[]{:S(2)}) collective-permute-start(f32[256,256]{1,0:T(8,128)S(1)} %get-tuple-element.12), channel_id=1, source_target_pairs={{1,0},{2,1},{3,2},{5,4},{6,5},{7,6},{9,8},{10,9},{11,10},{13,12},{... | collective-permute-start | bytes 786440 | tf_op jit(solution)/shard_map/ppermute | solution.py:23
  11.6 1.9 %collective-permute-start.2 = (f32[64,256]{1,0:T(8,128)S(1)}, f32[64,256]{1,0:T(8,128)S(1)}, u32[]{:S(2)}, u32[]{:S(2)}) collective-permute-start(f32[64,256]{1,0:T(8,128)S(1)} %get-tuple-element.13), channel_id=1, source_target_pairs={{0,4},{4,8},{8,12},{12,16},{16,20},{20,24},{24,28},{1,5},{5,9},{9,... | collective-permute-start | bytes 196616 | tf_op jit(solution)/shard_map/ppermute | solution.py:23
  13.6 3.6 %collective-permute-start.3 = (f32[64,256]{1,0:T(8,128)S(1)}, f32[64,256]{1,0:T(8,128)S(1)}, u32[]{:S(2)}, u32[]{:S(2)}) collective-permute-start(f32[64,256]{1,0:T(8,128)S(1)} %get-tuple-element.14), channel_id=1, source_target_pairs={{4,0},{8,4},{12,8},{16,12},{20,16},{24,20},{28,24},{5,1},{9,5},{13... | collective-permute-start | bytes 196616 | tf_op jit(solution)/shard_map/ppermute | solution.py:23
  17.2 3.8 %collective-permute-start.4 = (f32[128,128]{1,0:T(8,128)S(1)}, f32[128,128]{1,0:T(8,128)S(1)}, u32[]{:S(2)}, u32[]{:S(2)}) collective-permute-start(f32[128,128]{1,0:T(8,128)S(1)} %get-tuple-element.15), channel_id=1, source_target_pairs={{0,32},{32,64},{64,96},{1,33},{33,65},{65,97},{2,34},{34,66},{66,9... | collective-permute-start | bytes 196616 | tf_op jit(solution)/shard_map/ppermute | solution.py:23
  21.0 0.0 collective-permute-done.2.refs_7_
  21.1 2.0 %collective-permute-start.5 = (f32[128,128]{1,0:T(8,128)S(1)}, f32[128,128]{1,0:T(8,128)S(1)}, u32[]{:S(2)}, u32[]{:S(2)}) collective-permute-start(f32[128,128]{1,0:T(8,128)S(1)} %get-tuple-element.16), channel_id=1, source_target_pairs={{32,0},{64,32},{96,64},{33,1},{65,33},{97,65},{34,2},{66,34},{98,6... | collective-permute-start | bytes 196616 | tf_op jit(solution)/shard_map/ppermute | solution.py:23
  23.1 0.0 collective-permute-done.3.refs_8_
  23.1 0.3 collective-permute-done.4.refs_9_
  23.4 3.8 %collective-permute-done.5.refs_10_ = f32[128,128]{1,0:T(8,128)S(1)} collective-permute-done((f32[128,128]{1,0:T(8,128)S(1)}, f32[128,128]{1,0:T(8,128)S(1)}, u32[]{:S(2)}, u32[]{:S(2)}) %collective-permute-start.5) | collective-permute-done | bytes 65568 | tf_op jit(solution)/shard_map/ppermute | solution.py:23
  27.2 0.0 collective-permute-done.refs_5_
  27.2 0.0 collective-permute-done.1.refs_6_
  27.3 13.5 %march.5 = f32[8,64,256]{2,1,0:T(8,128)S(1)} custom-call(s32[4]{0:T(128)S(1)} %copy-done.1, s32[8]{0:T(128)S(1)} %copy-done.2, f32[3,8]{1,0:T(4,128)S(1)} %copy-done, f32[8]{0:T(128)S(1)} %copy-done.3, f32[64,256,256]{2,1,0:T(8,128)} %refs_4_.7, f32[256,256]{1,0:T(8,128)S(1)} %collective-permute-done.refs_5_, f32[256,256]{1,0:T(8,128)S(1)} %collective-permute-done.1.refs_6_, ...), custom_call_target="tpu_custom_call" | custom-call | flops 75497472 | bytes 4194304 | tf_op jit(solution)/shard_map/march/pallas_call | solution.py:296
  40.8 2.7 %collective-permute-start.6 = (f32[8,64,256]{2,1,0:T(8,128)S(1)}, f32[8,64,256]{2,1,0:T(8,128)S(1)}, u32[]{:S(2)}, u32[]{:S(2)}) collective-permute-start(f32[8,64,256]{2,1,0:T(8,128)S(1)} %march.5), channel_id=1, source_target_pairs={{0,1},{1,2},{2,3},{3,0},{4,5},{5,6},{6,7},{7,4},{8,9},{9,10},{10,1... | collective-permute-start | bytes 1572872 | tf_op jit(solution)/shard_map/ppermute | solution.py:28
  43.5 13.5 %march.6 = f32[8,64,256]{2,1,0:T(8,128)S(1)} custom-call(s32[4]{0:T(128)S(1)} %copy-done.1, s32[8]{0:T(128)S(1)} %copy-done.2, f32[3,8]{1,0:T(4,128)S(1)} %copy-done, f32[8]{0:T(128)S(1)} %copy-done.3, f32[64,256,256]{2,1,0:T(8,128)} %refs_4_.7, f32[256,256]{1,0:T(8,128)S(1)} %collective-permute-done.refs_5_, f32[256,256]{1,0:T(8,128)S(1)} %collective-permute-done.1.refs_6_, ...), custom_call_target="tpu_custom_call" | custom-call | flops 75497472 | bytes 4194304 | tf_op jit(solution)/shard_map/march/pallas_call | solution.py:296
  57.0 2.5 %collective-permute-start.7 = (f32[8,64,256]{2,1,0:T(8,128)S(1)}, f32[8,64,256]{2,1,0:T(8,128)S(1)}, u32[]{:S(2)}, u32[]{:S(2)}) collective-permute-start(f32[8,64,256]{2,1,0:T(8,128)S(1)} %march.6), channel_id=1, source_target_pairs={{0,2},{1,3},{2,0},{3,1},{4,6},{5,7},{6,4},{7,5},{8,10},{9,11},{10,... | collective-permute-start | bytes 1572872 | tf_op jit(solution)/shard_map/ppermute | solution.py:28
  59.5 13.5 %march.7 = f32[8,64,256]{2,1,0:T(8,128)S(1)} custom-call(s32[4]{0:T(128)S(1)} %copy-done.1, s32[8]{0:T(128)S(1)} %copy-done.2, f32[3,8]{1,0:T(4,128)S(1)} %copy-done, f32[8]{0:T(128)S(1)} %copy-done.3, f32[64,256,256]{2,1,0:T(8,128)} %refs_4_.7, f32[256,256]{1,0:T(8,128)S(1)} %collective-permute-done.refs_5_, f32[256,256]{1,0:T(8,128)S(1)} %collective-permute-done.1.refs_6_, ...), custom_call_target="tpu_custom_call" | custom-call | flops 75497472 | bytes 4194304 | tf_op jit(solution)/shard_map/march/pallas_call | solution.py:296
  73.0 1.8 %collective-permute-start.8 = (f32[8,64,256]{2,1,0:T(8,128)S(1)}, f32[8,64,256]{2,1,0:T(8,128)S(1)}, u32[]{:S(2)}, u32[]{:S(2)}) collective-permute-start(f32[8,64,256]{2,1,0:T(8,128)S(1)} %march.7), channel_id=1, source_target_pairs={{0,3},{1,0},{2,1},{3,2},{4,7},{5,4},{6,5},{7,6},{8,11},{9,8},{10,9... | collective-permute-start | bytes 1572872 | tf_op jit(solution)/shard_map/ppermute | solution.py:28
  74.8 13.4 %march.4.refs_1_ = f32[8,64,256]{2,1,0:T(8,128)S(1)} custom-call(s32[4]{0:T(128)S(1)} %copy-done.1, s32[8]{0:T(128)S(1)} %copy-done.2, f32[3,8]{1,0:T(4,128)S(1)} %copy-done, f32[8]{0:T(128)S(1)} %copy-done.3, f32[64,256,256]{2,1,0:T(8,128)} %refs_4_.7, f32[256,256]{1,0:T(8,128)S(1)} %collective-permute-done.refs_5_, ...), custom_call_target="tpu_custom_call" | custom-call | flops 75497472 | bytes 4194304 | tf_op jit(solution)/shard_map/march/pallas_call | solution.py:296
  88.2 0.0 collective-permute-done.6.refs_2_
  88.2 0.0 collective-permute-done.7.refs_3_
  88.2 0.0 collective-permute-done.8.refs_4_
  88.2 1.6 %compose.1 = f32[8,64,256]{2,1,0:T(8,128)} custom-call(s32[4]{0:T(128)S(1)} %copy-done.1, f32[8,64,256]{2,1,0:T(8,128)S(1)} %march.4.refs_1_, f32[8,64,256]{2,1,0:T(8,128)S(1)} %collective-permute-done.6.refs_2_, f32[8,64,256]{2,1,0:T(8,128)S(1)} %collective-permute-done.7.refs_3_, f32[8,64,256]{2,1,0:T(8,128)S(1)} %collective-permute-done.8.refs_4_), custom_call_target="tpu_custom_call" | custom-call | flops 1000000 | bytes 2621440 | tf_op jit(solution)/shard_map/compose/pallas_call | solution.py:350
  (8 shorter events, 0.0 us)
Async XLA Ops:
  0.0 27.2 %copy-start.1 = (s32[4]{0:T(128)S(1)}, s32[4]{0:T(128)}, u32[]{:S(2)}) copy-start(s32[4]{0:T(128)} %refs_0_.9) | copy-start | bytes 52
  0.0 27.2 %copy-start.3 = (f32[8]{0:T(128)S(1)}, f32[8]{0:T(128)}, u32[]{:S(2)}) copy-start(f32[8]{0:T(128)} %refs_3_.7) | copy-start | bytes 100
  0.0 27.2 %copy-start = (f32[3,8]{1,0:T(4,128)S(1)}, f32[3,8]{1,0:T(4,128)}, u32[]{:S(2)}) copy-start(f32[3,8]{1,0:T(4,128)} %refs_2_.7) | copy-start | bytes 292
  0.0 27.2 %copy-start.2 = (s32[8]{0:T(128)S(1)}, s32[8]{0:T(128)}, u32[]{:S(2)}) copy-start(s32[8]{0:T(128)} %refs_1_.7) | copy-start | bytes 100
  6.9 20.3 %collective-permute-start = (f32[256,256]{1,0:T(8,128)S(1)}, f32[256,256]{1,0:T(8,128)S(1)}, u32[]{:S(2)}, u32[]{:S(2)}) collective-permute-start(f32[256,256]{1,0:T(8,128)S(1)} %get-tuple-element.11), channel_id=1, source_target_pairs={{0,1},{1,2},{2,3},{4,5},{5,6},{6,7},{8,9},{9,10},{10,11},{12,13},{... | collective-permute-start | bytes 786440 | tf_op jit(solution)/shard_map/ppermute | solution.py:23
  10.3 16.9 %collective-permute-start.1 = (f32[256,256]{1,0:T(8,128)S(1)}, f32[256,256]{1,0:T(8,128)S(1)}, u32[]{:S(2)}, u32[]{:S(2)}) collective-permute-start(f32[256,256]{1,0:T(8,128)S(1)} %get-tuple-element.12), channel_id=1, source_target_pairs={{1,0},{2,1},{3,2},{5,4},{6,5},{7,6},{9,8},{10,9},{11,10},{13,12},{... | collective-permute-start | bytes 786440 | tf_op jit(solution)/shard_map/ppermute | solution.py:23
  11.6 9.4 %collective-permute-start.2 = (f32[64,256]{1,0:T(8,128)S(1)}, f32[64,256]{1,0:T(8,128)S(1)}, u32[]{:S(2)}, u32[]{:S(2)}) collective-permute-start(f32[64,256]{1,0:T(8,128)S(1)} %get-tuple-element.13), channel_id=1, source_target_pairs={{0,4},{4,8},{8,12},{12,16},{16,20},{20,24},{24,28},{1,5},{5,9},{9,... | collective-permute-start | bytes 196616 | tf_op jit(solution)/shard_map/ppermute | solution.py:23
  13.6 9.5 %collective-permute-start.3 = (f32[64,256]{1,0:T(8,128)S(1)}, f32[64,256]{1,0:T(8,128)S(1)}, u32[]{:S(2)}, u32[]{:S(2)}) collective-permute-start(f32[64,256]{1,0:T(8,128)S(1)} %get-tuple-element.14), channel_id=1, source_target_pairs={{4,0},{8,4},{12,8},{16,12},{20,16},{24,20},{28,24},{5,1},{9,5},{13... | collective-permute-start | bytes 196616 | tf_op jit(solution)/shard_map/ppermute | solution.py:23
  17.2 6.2 %collective-permute-start.4 = (f32[128,128]{1,0:T(8,128)S(1)}, f32[128,128]{1,0:T(8,128)S(1)}, u32[]{:S(2)}, u32[]{:S(2)}) collective-permute-start(f32[128,128]{1,0:T(8,128)S(1)} %get-tuple-element.15), channel_id=1, source_target_pairs={{0,32},{32,64},{64,96},{1,33},{33,65},{65,97},{2,34},{34,66},{66,9... | collective-permute-start | bytes 196616 | tf_op jit(solution)/shard_map/ppermute | solution.py:23
  21.1 6.2 %collective-permute-start.5 = (f32[128,128]{1,0:T(8,128)S(1)}, f32[128,128]{1,0:T(8,128)S(1)}, u32[]{:S(2)}, u32[]{:S(2)}) collective-permute-start(f32[128,128]{1,0:T(8,128)S(1)} %get-tuple-element.16), channel_id=1, source_target_pairs={{32,0},{64,32},{96,64},{33,1},{65,33},{97,65},{34,2},{66,34},{98,6... | collective-permute-start | bytes 196616 | tf_op jit(solution)/shard_map/ppermute | solution.py:23
  40.8 47.4 %collective-permute-start.6 = (f32[8,64,256]{2,1,0:T(8,128)S(1)}, f32[8,64,256]{2,1,0:T(8,128)S(1)}, u32[]{:S(2)}, u32[]{:S(2)}) collective-permute-start(f32[8,64,256]{2,1,0:T(8,128)S(1)} %march.5), channel_id=1, source_target_pairs={{0,1},{1,2},{2,3},{3,0},{4,5},{5,6},{6,7},{7,4},{8,9},{9,10},{10,1... | collective-permute-start | bytes 1572872 | tf_op jit(solution)/shard_map/ppermute | solution.py:28
  57.0 31.2 %collective-permute-start.7 = (f32[8,64,256]{2,1,0:T(8,128)S(1)}, f32[8,64,256]{2,1,0:T(8,128)S(1)}, u32[]{:S(2)}, u32[]{:S(2)}) collective-permute-start(f32[8,64,256]{2,1,0:T(8,128)S(1)} %march.6), channel_id=1, source_target_pairs={{0,2},{1,3},{2,0},{3,1},{4,6},{5,7},{6,4},{7,5},{8,10},{9,11},{10,... | collective-permute-start | bytes 1572872 | tf_op jit(solution)/shard_map/ppermute | solution.py:28
  73.0 15.2 %collective-permute-start.8 = (f32[8,64,256]{2,1,0:T(8,128)S(1)}, f32[8,64,256]{2,1,0:T(8,128)S(1)}, u32[]{:S(2)}, u32[]{:S(2)}) collective-permute-start(f32[8,64,256]{2,1,0:T(8,128)S(1)} %march.7), channel_id=1, source_target_pairs={{0,3},{1,0},{2,1},{3,2},{4,7},{5,4},{6,5},{7,6},{8,11},{9,8},{10,9... | collective-permute-start | bytes 1572872 | tf_op jit(solution)/shard_map/ppermute | solution.py:28
